TPU v7x, 1024 devices: a whole 4x8x16 slice. The times are simulated.
1024 devices in a mesh: tile: 128 (over y, z), depth: 8 (over x, core).
Axes of the slice: x: 4, y: 8, z: 16, core: 2. Of those that a mesh axis runs over, the one named last changes fastest.
Arguments:
- volume: bfloat16 [2048, 256, 2048], P('tile', 'depth'), may hold values from -4 to 4
Outputs:
- image: float32 [4, 2048, 2048], P(None, ('tile', 'depth'))
All inputs are finite; a program needn't handle non-finite values.
Results may differ from a plain program's by a relative error of at most 0.0003.
Values may be sent and summed in bfloat16 or wider, within the bound.
A program may use at most 32 MiB of HBM per device.

v0:
```python
import jax
import jax.numpy as jnp
from jax import lax
from jax.sharding import PartitionSpec as P

OPACITY = 3.0
LIGHT_X = 0.48
LIGHT_Y = 0.6
LIGHT_Z = 0.64


def padded_2(block, sides, width):
    for axis, dim in sides:
        count = lax.axis_size(axis)
        forward = [(i, i + 1) for i in range(count - 1)]
        backward = [(target, source) for source, target in forward]
        low = lax.ppermute(
            lax.slice_in_dim(block, block.shape[dim] - width, None, axis=dim), axis, forward
        )
        high = lax.ppermute(lax.slice_in_dim(block, 0, width, axis=dim), axis, backward)
        block = jnp.concatenate([low, block, high], axis=dim)
    return block


def brick_image(padded, depth_total):
    field = padded.astype(jnp.float32)
    center = field[1:-1, 1:-1, 1:-1]
    grad_x = 0.5 * (field[2:, 1:-1, 1:-1] - field[:-2, 1:-1, 1:-1])
    grad_z = 0.5 * (field[1:-1, 2:, 1:-1] - field[1:-1, :-2, 1:-1])
    grad_y = 0.5 * (field[1:-1, 1:-1, 2:] - field[1:-1, 1:-1, :-2])
    facing = LIGHT_X * grad_x + LIGHT_Y * grad_y + LIGHT_Z * grad_z
    shade = 0.3 + 0.7 * jnp.abs(facing) / jnp.sqrt(
        1.0 + grad_x * grad_x + grad_y * grad_y + grad_z * grad_z
    )
    squared = center * center
    extinct = OPACITY / depth_total * squared / (1.0 + squared)
    before = jnp.cumsum(extinct, axis=1) - extinct
    weight = jnp.exp(-before) * (1.0 - jnp.exp(-extinct)) * shade
    red = jnp.sum(weight * jax.nn.sigmoid(2.0 * center), axis=1)
    green = jnp.sum(weight * (0.5 * jnp.exp(-squared)), axis=1)
    blue = jnp.sum(weight * jax.nn.sigmoid(-2.0 * center), axis=1)
    passing = jnp.exp(-jnp.sum(extinct, axis=1))
    return jnp.stack([red, green, blue, passing], 0)


def shards(volume):
    depth_count = lax.axis_size("depth")
    cells_x = volume.shape[0]
    rows_y = volume.shape[2]
    pieces = cells_x // depth_count
    depth_total = volume.shape[1] * depth_count
    extended = padded_2(volume, (("tile", 0), ("depth", 1)), 1)
    extended = jnp.pad(extended, ((0, 0), (0, 0), (1, 1)))
    part = brick_image(extended, depth_total)
    received = lax.all_to_all(part[None], "depth", split_axis=2, concat_axis=0, tiled=True)

    def blend(carry, piece):
        colour, passing = carry
        return ((colour + passing * piece[:3], passing * piece[3:]), None)

    start = (
        jnp.zeros((3, pieces, rows_y), jnp.float32),
        jnp.ones((1, pieces, rows_y), jnp.float32),
    )
    (colour, passing), _ = lax.scan(blend, start, received)
    return jnp.concatenate([colour, 1.0 - passing], 0)


def solution(mesh):
    in_specs = (P("tile", "depth", None),)
    out_specs = P(None, ("tile", "depth"), None)
    return jax.shard_map(shards, mesh=mesh, in_specs=in_specs, out_specs=out_specs, check_vma=False)
```

profile of v0, /device:TPU:56, one launch (start us, length us, event | category | flops | bytes accessed | tf_op | source)
XLA Modules:
  0.0 75.3 jit_solution(9334768992461896646)
XLA Ops:
  0.0 2.7 %copy.9 = bf16[16,32,2048]{2,0,1:T(8,128)(2,1)S(1)} copy(bf16[16,32,2048]{2,1,0:T(8,128)(2,1)} %param.3) | data formatting | bytes 4194304 | tf_op args[0]
  2.7 0.4 fusion.13
  3.2 4.3 %collective-permute-start = (bf16[1,32,2048]{2,0,1:T(2,128)(2,1)S(1)}, bf16[1,32,2048]{2,0,1:T(2,128)(2,1)S(1)}, u32[]{:S(2)}, u32[]{:S(2)}) collective-permute-start(bf16[1,32,2048]{2,0,1:T(2,128)(2,1)S(1)} %get-tuple-element.69), channel_id=1, source_target_pairs={{0,8},{8,16},{16,24},{24,32},{32,40},{40,48},{48,56},{56,64},{64,7... | collective-permute-start | bytes 393224 | tf_op jit(solution)/shard_map/ppermute | solution.py:17
  7.5 16.6 %collective-permute-start.1 = (bf16[1,32,2048]{2,0,1:T(2,128)(2,1)S(1)}, bf16[1,32,2048]{2,0,1:T(2,128)(2,1)S(1)}, u32[]{:S(2)}, u32[]{:S(2)}) collective-permute-start(bf16[1,32,2048]{2,0,1:T(2,128)(2,1)S(1)} %get-tuple-element.70), channel_id=1, source_target_pairs={{8,0},{16,8},{24,16},{32,24},{40,32},{48,40},{56,48},{64,56},{72,6... | collective-permute-start | bytes 393224 | tf_op jit(solution)/shard_map/ppermute | solution.py:20
  24.1 4.4 %collective-permute-done = bf16[1,32,2048]{2,0,1:T(2,128)(2,1)S(1)} collective-permute-done((bf16[1,32,2048]{2,0,1:T(2,128)(2,1)S(1)}, bf16[1,32,2048]{2,0,1:T(2,128)(2,1)S(1)}, u32[]{:S(2)}, u32[]{:S(2)}) %collective-permute-start) | collective-permute-done | bytes 131104 | tf_op jit(solution)/shard_map/ppermute | solution.py:17
  28.5 1.2 %collective-permute-done.1 = bf16[1,32,2048]{2,0,1:T(2,128)(2,1)S(1)} collective-permute-done((bf16[1,32,2048]{2,0,1:T(2,128)(2,1)S(1)}, bf16[1,32,2048]{2,0,1:T(2,128)(2,1)S(1)}, u32[]{:S(2)}, u32[]{:S(2)}) %collective-permute-start.1) | collective-permute-done | bytes 131104 | tf_op jit(solution)/shard_map/ppermute | solution.py:20
  29.7 0.1 pad_maximum_fusion.2
  29.7 1.3 %collective-permute-start.2 = (bf16[18,1,2048]{2,0,1:T(8,128)(2,1)S(1)}, bf16[18,1,2048]{2,0,1:T(8,128)(2,1)S(1)}, u32[]{:S(2)}, u32[]{:S(2)}) collective-permute-start(bf16[18,1,2048]{2,0,1:T(8,128)(2,1)S(1)} %get-tuple-element.67), channel_id=1, source_target_pairs={{0,1},{1,2},{2,3},{3,4},{4,5},{5,6},{6,7},{8,9},{9,10},{10,11},{11... | collective-permute-start | bytes 221192 | tf_op jit(solution)/shard_map/ppermute | solution.py:17
  31.1 1.3 %collective-permute-start.3 = (bf16[18,1,2048]{2,0,1:T(8,128)(2,1)S(1)}, bf16[18,1,2048]{2,0,1:T(8,128)(2,1)S(1)}, u32[]{:S(2)}, u32[]{:S(2)}) collective-permute-start(bf16[18,1,2048]{2,0,1:T(8,128)(2,1)S(1)} %get-tuple-element.68), channel_id=1, source_target_pairs={{1,0},{2,1},{3,2},{4,3},{5,4},{6,5},{7,6},{9,8},{10,9},{11,10},{12... | collective-permute-start | bytes 221192 | tf_op jit(solution)/shard_map/ppermute | solution.py:20
  32.4 0.0 collective-permute-done.2
  32.4 3.6 %collective-permute-done.3 = bf16[18,1,2048]{2,0,1:T(8,128)(2,1)S(1)} collective-permute-done((bf16[18,1,2048]{2,0,1:T(8,128)(2,1)S(1)}, bf16[18,1,2048]{2,0,1:T(8,128)(2,1)S(1)}, u32[]{:S(2)}, u32[]{:S(2)}) %collective-permute-start.3) | collective-permute-done | bytes 73760 | tf_op jit(solution)/shard_map/ppermute | solution.py:20
  36.0 5.5 %fusion.5 = f32[18,34,2050]{2,0,1:T(8,128)S(1)} fusion(bf16[18,1,2048]{2,0,1:T(8,128)(2,1)S(1)} %collective-permute-done.3, bf16[18,1,2048]{2,0,1:T(8,128)(2,1)S(1)} %collective-permute-done.2, bf16[1,32,2048]{2,0,1:T(2,128)(2,1)S(1)} %collective-permute-done.1, bf16[16,32,2048]{2,0,1:T(8,128)(2,1)S(1)} %copy.9, bf16[1,32,2048]{2,0,1:T(2,128)(2,1)S(1)} %collective-permute-done), kind=kLoop, calls=%fused_computation.21 | loop fusion | flops 22582800 | bytes 7525152 | tf_op jit(solution)/shard_map/convert_element_type | solution.py:26
  41.5 12.9 %multiply_reduce_fusion.2 = (f32[16,2048]{1,0:T(8,128)S(1)}, f32[16,2048]{1,0:T(8,128)S(1)}, f32[16,2048]{1,0:T(8,128)S(1)}, f32[16,2048]{1,0:T(8,128)S(1)}) fusion(f32[18,34,2050]{2,0,1:T(8,128)S(1)} %fusion.5), kind=kOutput, calls=%fused_computation.17 | output fusion | flops 86900736 | bytes 34078720 | tf_op jit(solution)/shard_map/jit(cumsum)/reduce_window_sum | solution.py:37
  54.4 0.1 exp.34
  54.5 0.1 stack.13
  54.6 0.1 stack.14
  54.7 0.1 stack.15
  54.8 1.3 %maximum_bitcast_fusion = f32[1,4,16,2048]{3,1,0,2:T(4,128)} fusion(f32[1,16,2048]{2,0,1:T(1,128)S(1)} %exp.34, f32[1,16,2048]{2,0,1:T(1,128)S(1)} %stack.15, f32[1,16,2048]{2,0,1:T(1,128)S(1)} %stack.14, f32[1,16,2048]{2,0,1:T(1,128)S(1)} %stack.13), kind=kLoop, calls=%fused_computation.28 | loop fusion | flops 393216 | bytes 1048576 | tf_op jit(solution)/shard_map/broadcast_in_dim | solution.py:55
  56.0 6.8 %all-to-all-start = ((f32[1,4,16,2048]{3,1,0,2:T(4,128)}), f32[1,4,16,2048]{3,1,0,2:T(4,128)S(1)}, u32[]{:S(2)}, u32[]{:S(2)}) async-start(f32[1,4,16,2048]{3,1,0,2:T(4,128)} %maximum_bitcast_fusion), calls=%async_computation | async-start | bytes 1048576 | tf_op jit(solution)/shard_map/all_to_all | solution.py:55
  62.9 10.3 %all-to-all-done = f32[1,4,16,2048]{3,1,0,2:T(4,128)S(1)} async-done(((f32[1,4,16,2048]{3,1,0,2:T(4,128)}), f32[1,4,16,2048]{3,1,0,2:T(4,128)S(1)}, u32[]{:S(2)}, u32[]{:S(2)}) %all-to-all-start) | async-done | bytes 524320 | tf_op jit(solution)/shard_map/all_to_all | solution.py:55
  73.2 1.4 %while.13 = (s32[]{:T(128)}, f32[3,2,2048]{2,1,0:T(2,128)S(1)}, f32[1,2,2048]{2,1,0:T(2,128)S(1)}, f32[8,4,2,2048]{3,1,2,0:T(4,128)S(1)}, s32[]{:T(128)}, /*index=5*/s32[]{:T(128)}, s32[]{}) while((s32[]{:T(128)}, f32[3,2,2048]{2,1,0:T(2,128)S(1)}, f32[1,2,2048]{2,1,0:T(2,128)S(1)}, f32[8,4,2,2048]{3,1,2,0:T(4,128)S(1)}, ...), condition=%wide.region_6.7_spmd.clone, body=%wide.region_5.6_spmd.clone.sunk | while | flops 45060 | bytes 360560 | solution.py:65
  73.3 0.1 fusion.17
  73.5 0.1 fusion.17
  73.7 0.1 fusion.17
  73.9 0.1 fusion.17
  74.0 0.1 fusion.17
  74.2 0.1 fusion.17
  74.4 0.1 fusion.17
  74.6 0.1 fusion.17
  74.7 0.7 pad_maximum_fusion.3
  (28 shorter events, 0.6 us)
Async XLA Ops:
  3.2 25.3 %collective-permute-start = (bf16[1,32,2048]{2,0,1:T(2,128)(2,1)S(1)}, bf16[1,32,2048]{2,0,1:T(2,128)(2,1)S(1)}, u32[]{:S(2)}, u32[]{:S(2)}) collective-permute-start(bf16[1,32,2048]{2,0,1:T(2,128)(2,1)S(1)} %get-tuple-element.69), channel_id=1, source_target_pairs={{0,8},{8,16},{16,24},{24,32},{32,40},{40,48},{48,56},{56,64},{64,7... | collective-permute-start | bytes 393224 | tf_op jit(solution)/shard_map/ppermute | solution.py:17
  7.5 22.2 %collective-permute-start.1 = (bf16[1,32,2048]{2,0,1:T(2,128)(2,1)S(1)}, bf16[1,32,2048]{2,0,1:T(2,128)(2,1)S(1)}, u32[]{:S(2)}, u32[]{:S(2)}) collective-permute-start(bf16[1,32,2048]{2,0,1:T(2,128)(2,1)S(1)} %get-tuple-element.70), channel_id=1, source_target_pairs={{8,0},{16,8},{24,16},{32,24},{40,32},{48,40},{56,48},{64,56},{72,6... | collective-permute-start | bytes 393224 | tf_op jit(solution)/shard_map/ppermute | solution.py:20
  29.7 2.6 %collective-permute-start.2 = (bf16[18,1,2048]{2,0,1:T(8,128)(2,1)S(1)}, bf16[18,1,2048]{2,0,1:T(8,128)(2,1)S(1)}, u32[]{:S(2)}, u32[]{:S(2)}) collective-permute-start(bf16[18,1,2048]{2,0,1:T(8,128)(2,1)S(1)} %get-tuple-element.67), channel_id=1, source_target_pairs={{0,1},{1,2},{2,3},{3,4},{4,5},{5,6},{6,7},{8,9},{9,10},{10,11},{11... | collective-permute-start | bytes 221192 | tf_op jit(solution)/shard_map/ppermute | solution.py:17
  31.1 4.9 %collective-permute-start.3 = (bf16[18,1,2048]{2,0,1:T(8,128)(2,1)S(1)}, bf16[18,1,2048]{2,0,1:T(8,128)(2,1)S(1)}, u32[]{:S(2)}, u32[]{:S(2)}) collective-permute-start(bf16[18,1,2048]{2,0,1:T(8,128)(2,1)S(1)} %get-tuple-element.68), channel_id=1, source_target_pairs={{1,0},{2,1},{3,2},{4,3},{5,4},{6,5},{7,6},{9,8},{10,9},{11,10},{12... | collective-permute-start | bytes 221192 | tf_op jit(solution)/shard_map/ppermute | solution.py:20
  56.0 17.2 %all-to-all-start = ((f32[1,4,16,2048]{3,1,0,2:T(4,128)}), f32[1,4,16,2048]{3,1,0,2:T(4,128)S(1)}, u32[]{:S(2)}, u32[]{:S(2)}) async-start(f32[1,4,16,2048]{3,1,0,2:T(4,128)} %maximum_bitcast_fusion), calls=%async_computation | async-start | bytes 1048576 | tf_op jit(solution)/shard_map/all_to_all | solution.py:55
where the time goes:
time: 75.6 us; the launch traced here: 75.3 us
  starting transfers between devices  30.4 us (40%)
  other arithmetic  21.2 us (28%)
  waiting for transfers between devices  19.5 us (26%)
  local copies, waits for them, and re-layouts  3.83 us (5%)
    ppermute x2, starting transfers between devices, padded_2(): lax.ppermute(lax.slice_in_dim(block, 0, width, axis=dim), axis, backward)  17.9 us
    another operation x1, other arithmetic, brick_image(): before = jnp.cumsum(extinct, axis=1) - extinct  12.9 us
    all_to_all x1, waiting for transfers between devices, shards(): lax.all_to_all(part[None], 'depth', split_axis=2, concat_axis=0, tiled=True)  10.3 us
    all_to_all x1, starting transfers between devices, shards(): lax.all_to_all(part[None], 'depth', split_axis=2, concat_axis=0, tiled=True)  6.85 us
    ppermute x2, starting transfers between devices, padded_2(): lax.ppermute(lax.slice_in_dim(block, block.shape[dim] - width, None, axis...  5.58 us
    convert_element_type x1, other arithmetic, brick_image(): field = padded.astype(jnp.float32)  5.48 us
    ppermute x2, waiting for transfers between devices, padded_2(): lax.ppermute(lax.slice_in_dim(block, 0, width, axis=dim), axis, backward)  4.79 us
    ppermute x2, waiting for transfers between devices, padded_2(): lax.ppermute(lax.slice_in_dim(block, block.shape[dim] - width, None, axis...  4.36 us
  transfers between devices with their start and end apart: 5, of which 4 were waited for; matrix products, arithmetic and copies ran while one was open for 0% of the time, Pallas kernels for 0%

commit v1 on v0

v1 whole, which is shorter than its diff:
```python
import functools
import math

import jax
import jax.numpy as jnp
from jax import lax
from jax.experimental import pallas as pl
from jax.experimental.pallas import tpu as pltpu
from jax.sharding import PartitionSpec as P

OPACITY = 3.0
LIGHT_X = 0.48
LIGHT_Y = 0.6
LIGHT_Z = 0.64
LOG2E = math.log2(math.e)
SHADE = 0.7 * LIGHT_Z
UNROLL = 4


def column_terms(rate, centre, x_pair, y_diff, z_pair, state):
    run, light, total, skew, green = state
    gx = x_pair[1] - x_pair[0]
    gz = z_pair[1] - z_pair[0]
    gy = y_diff
    facing = jnp.abs(gz + (LIGHT_X / LIGHT_Z) * gx + (LIGHT_Y / LIGHT_Z) * gy)
    norm = lax.rsqrt((gx * gx + 4.0) + (gy * gy + gz * gz))
    shade = facing * norm + 0.3 / SHADE
    squared = centre * centre
    run = run + squared * pl_reciprocal(1.0 + squared)
    after = jnp.exp2(run * (-rate))
    weight = (light - after) * shade
    total = total + weight
    skew = skew + weight * jnp.tanh(centre)
    green = green + weight * jnp.exp2(squared * (-LOG2E))
    return run, after, total, skew, green


def pl_reciprocal(value):
    return pltpu.reciprocal(value, approx=True)


def y_differences(first, second, lane, row):
    above = jnp.where(row == 7, 0.0, pltpu.roll(first, 7, 0))
    below = jnp.where(row == 0, 0.0, pltpu.roll(second, 1, 0))
    right_0 = pltpu.roll(jnp.where(lane == 0, second, first), 127, 1)
    right_1 = pltpu.roll(jnp.where(lane == 0, above, second), 127, 1)
    left_0 = pltpu.roll(jnp.where(lane == 127, below, first), 1, 1)
    left_1 = pltpu.roll(jnp.where(lane == 127, first, second), 1, 1)
    return right_0 - left_0, right_1 - left_1


def relayout(order, slab):
    stacked = jnp.concatenate([slab[:, 256 * c : 256 * c + 256] for c in range(8)], axis=0)
    return jnp.dot(order, stacked, preferred_element_type=jnp.float32)


def render_kernel(
    tiles, depths, v_ref, o_ref, vin, ws, zout, zin, part, recv,
    load_sem, xs_sem, xr_sem, zs_sem, zr_sem, ps_sem, pr_sem,
):
    MESH = pl.DeviceIdType.MESH
    cx, cz, _ = v_ref.shape
    tile = lax.axis_index("tile")
    me = lax.axis_index("depth")
    tile_up, tile_down = lax.rem(tile + 1, tiles), lax.rem(tile + tiles - 1, tiles)
    deep_up, deep_down = lax.rem(me + 1, depths), lax.rem(me + depths - 1, depths)
    rate = OPACITY / (cz * depths) * LOG2E

    barrier = pltpu.get_barrier_semaphore()
    for other in (tile_up, tile_down):
        pl.semaphore_signal(barrier, inc=1, device_id={"tile": other}, device_id_type=MESH)
    for step in range(1, depths):
        pl.semaphore_signal(
            barrier, inc=1, device_id={"depth": lax.rem(me + step, depths)}, device_id_type=MESH
        )
    loads = []
    for i in range(4):
        n = cx // 4
        loads.append(
            pltpu.make_async_copy(
                v_ref.at[pl.ds(i * n, n)], vin.at[pl.ds(1 + i * n, n)], load_sem.at[i]
            )
        )
        loads[-1].start()
    in_row = lax.broadcasted_iota(jnp.int32, (256, 256), 1)
    out_row = lax.broadcasted_iota(jnp.int32, (256, 256), 0)
    wanted = (out_row % 8) * 32 + out_row // 8
    order = jnp.where(in_row == wanted, 1.0, 0.0).astype(jnp.bfloat16)

    pl.semaphore_wait(barrier, depths + 1)
    x_down = pltpu.make_async_remote_copy(
        v_ref.at[0], vin.at[cx + 1], xs_sem.at[0], xr_sem.at[0],
        device_id={"tile": tile_down}, device_id_type=MESH,
    )
    x_up = pltpu.make_async_remote_copy(
        v_ref.at[cx - 1], vin.at[0], xs_sem.at[1], xr_sem.at[1],
        device_id={"tile": tile_up}, device_id_type=MESH,
    )
    x_down.start()
    x_up.start()

    def own_slab(x, _):
        ws[x, pl.ds(8, 256), :] = relayout(order, vin[x])
        return 0

    for i in range(4):
        loads[i].wait()
        lax.fori_loop(1 + i * (cx // 4), 1 + (i + 1) * (cx // 4), own_slab, 0)

    def pack(x, _):
        for side, z in ((0, 1), (1, cz)):
            rows = ws[x + 1, pl.ds(8 * z, 8), :]
            zout[side, x] = jnp.concatenate([rows[:, :128], rows[:, 128:]], axis=0).astype(jnp.bfloat16)
        return 0

    lax.fori_loop(0, cx, pack, 0)
    z_down = pltpu.make_async_remote_copy(
        zout.at[0], zin.at[1], zs_sem.at[0], zr_sem.at[0],
        device_id={"depth": deep_down}, device_id_type=MESH,
    )
    z_up = pltpu.make_async_remote_copy(
        zout.at[1], zin.at[0], zs_sem.at[1], zr_sem.at[1],
        device_id={"depth": deep_up}, device_id_type=MESH,
    )
    z_down.start()
    z_up.start()

    x_down.wait_recv()
    x_up.wait_recv()
    keep_high = jnp.where(tile == tiles - 1, 0.0, 1.0)
    keep_low = jnp.where(tile == 0, 0.0, 1.0)
    ws[0, pl.ds(8, 256), :] = relayout(order, vin[0]) * keep_low
    ws[cx + 1, pl.ds(8, 256), :] = relayout(order, vin[cx + 1]) * keep_high
    z_down.wait_recv()
    z_up.wait_recv()
    near = jnp.where(me == 0, 0.0, 1.0)
    far = jnp.where(me == depths - 1, 0.0, 1.0)

    def unpack(x, _):
        for side, z, keep in ((0, 0, near), (1, cz + 1, far)):
            rows = zin[side, x].astype(jnp.float32) * keep
            ws[x + 1, pl.ds(8 * z, 8), :] = jnp.concatenate([rows[:8], rows[8:]], axis=1)
        return 0

    lax.fori_loop(0, cx, unpack, 0)

    lane = lax.broadcasted_iota(jnp.int32, (8, 128), 1)
    row = lax.broadcasted_iota(jnp.int32, (8, 128), 0)

    def group(d):
        first = 2 * d

        def cell(slab, z, h):
            start = 8 * z if isinstance(z, int) else pl.multiple_of(8 * z, 8)
            return ws[first + slab, pl.ds(start, 8), 128 * h : 128 * h + 128]

        def body(i, state):
            state = list(state)
            for u in range(UNROLL):
                z = i * UNROLL + u + 1
                for x in range(2):
                    centre = [cell(x + 1, z, h) for h in range(2)]
                    gy = y_differences(centre[0], centre[1], lane, row)
                    for h in range(2):
                        at = 2 * x + h
                        state[at] = column_terms(
                            rate,
                            centre[h],
                            (cell(x, z, h), cell(x + 2, z, h)),
                            gy[h],
                            (cell(x + 1, z - 1, h), cell(x + 1, z + 1, h)),
                            state[at],
                        )
            return tuple(state)

        zero = jnp.zeros((8, 128), jnp.float32)
        one = jnp.ones((8, 128), jnp.float32)
        state = tuple((zero, one, zero, zero, zero) for _ in range(4))
        state = lax.fori_loop(0, cz // UNROLL, body, state)
        for x in range(2):
            for h in range(2):
                run, _, total, skew, green = state[2 * x + h]
                for channel, value in enumerate((total, skew, green, run)):
                    part[d, channel, x, :, 128 * h : 128 * h + 128] = value

    def send(d):
        return pltpu.make_async_remote_copy(
            part.at[d], recv.at[me], ps_sem.at[d], pr_sem.at[me],
            device_id={"depth": d}, device_id_type=MESH,
        )

    def step(s, _):
        d = lax.rem(me + 1 + s, depths)
        group(d)

        @pl.when(s < depths - 1)
        def _():
            send(d).start()

        return 0

    lax.fori_loop(0, depths, step, 0)
    recv[me] = part[me]

    for s in range(1, depths):
        source = lax.rem(me + s, depths)
        pltpu.make_async_remote_copy(
            part.at[source], recv.at[source], ps_sem.at[source], pr_sem.at[source],
            device_id={"depth": source}, device_id_type=MESH,
        ).wait_recv()

    for x in range(2):
        run = recv[0, 3, x]
        total, skew, green = recv[0, 0, x], recv[0, 1, x], recv[0, 2, x]
        for k in range(1, depths):
            light = jnp.exp2(run * (-rate))
            total = total + light * recv[k, 0, x]
            skew = skew + light * recv[k, 1, x]
            green = green + light * recv[k, 2, x]
            run = run + recv[k, 3, x]
        half = 0.5 * SHADE
        o_ref[0, x] = half * (total + skew)
        o_ref[1, x] = half * green
        o_ref[2, x] = half * (total - skew)
        o_ref[3, x] = 1.0 - jnp.exp2(run * (-rate))

    x_down.wait_send()
    x_up.wait_send()
    z_down.wait_send()
    z_up.wait_send()
    for s in range(1, depths):
        send(lax.rem(me + s, depths)).wait_send()


def shards(volume):
    tiles, depths = lax.axis_size("tile"), lax.axis_size("depth")
    cx, cz, ny = volume.shape
    dma = pltpu.SemaphoreType.DMA
    image = pl.pallas_call(
        functools.partial(render_kernel, tiles, depths),
        out_shape=jax.ShapeDtypeStruct((4, cx // depths, 8, ny // 8), jnp.float32),
        in_specs=[pl.BlockSpec(memory_space=pltpu.HBM)],
        out_specs=pl.BlockSpec(memory_space=pltpu.VMEM),
        scratch_shapes=[
            pltpu.VMEM((cx + 2, cz, ny), jnp.bfloat16),
            pltpu.VMEM((cx + 2, 8 * (cz + 2), 256), jnp.float32),
            pltpu.VMEM((2, cx, 16, 128), jnp.bfloat16),
            pltpu.VMEM((2, cx, 16, 128), jnp.bfloat16),
            pltpu.VMEM((depths, 4, 2, 8, 256), jnp.float32),
            pltpu.VMEM((depths, 4, 2, 8, 256), jnp.float32),
            dma((4,)), dma((2,)), dma((2,)), dma((2,)), dma((2,)), dma((depths,)), dma((depths,)),
        ],
        compiler_params=pltpu.CompilerParams(
            collective_id=0, has_side_effects=True, vmem_limit_bytes=61 * 1024 * 1024
        ),
        cost_estimate=pl.CostEstimate(flops=50_000_000, bytes_accessed=2_300_000, transcendentals=5_000_000),
    )(volume)
    return image.reshape(4, cx // depths, ny)


def solution(mesh):
    in_specs = (P("tile", "depth", None),)
    out_specs = P(None, ("tile", "depth"), None)
    return jax.shard_map(shards, mesh=mesh, in_specs=in_specs, out_specs=out_specs, check_vma=False)
```

time: 75.6 us -> 41.6 us (0.55)
  the two profiles are of different devices: /device:TPU:56 before, /device:TPU:1 now
where the time goes in v1:
time: 41.6 us; the launch traced here: 41.4 us
  Pallas kernels  39.9 us (96%)
  local copies, waits for them, and re-layouts  1.51 us (4%)
    pallas_call x1, Pallas kernels, shards(): pl.pallas_call(functools.partial(render_kernel, tiles, depths), out_shape...  39.9 us
    reshape x1, local copies, waits for them, and re-layouts, shards(): return image.reshape(4, cx // depths, ny)  1.51 us

profile of v1, /device:TPU:1, one launch (start us, length us, event | category | flops | bytes accessed | tf_op | source)
XLA Modules:
  0.0 41.4 jit_solution(40658051204724697)
XLA Ops:
  0.0 39.9 %shard_map.17 = f32[4,2,8,256]{3,2,1,0:T(8,128)} custom-call(bf16[16,32,2048]{2,1,0:T(8,128)(2,1)} %v_ref.1), custom_call_target="tpu_custom_call" | custom-call | flops 50000000 | bytes 2300000 | tf_op jit(solution)/shard_map/pallas_call | solution.py:239
  39.9 1.5 %reshape.3 = f32[4,2,2048]{2,1,0:T(2,128)} reshape(f32[4,2,8,256]{3,2,1,0:T(8,128)} %shard_map.17) | data formatting | bytes 131072 | tf_op jit(solution)/shard_map/reshape | solution.py:258

commit v2 on v1

v2 whole, which is shorter than its diff:
```python
import functools
import math

import jax
import jax.numpy as jnp
from jax import lax
from jax.experimental import pallas as pl
from jax.experimental.pallas import tpu as pltpu
from jax.sharding import PartitionSpec as P

OPACITY = 3.0
LIGHT_X = 0.48
LIGHT_Y = 0.6
LIGHT_Z = 0.64
LOG2E = math.log2(math.e)
SHADE = 0.7 * LIGHT_Z
PITCH = 16
LEAD = 8
EARLY = 3
MESH = pl.DeviceIdType.MESH


def plan(depths):
    early = min(EARLY, depths - 2)
    use = {}
    orders = []
    for me in range(depths):
        left = [(me + s) % depths for s in range(1, depths)]
        order = []
        for step in range(depths - 1):
            allowed = [d for d in left if step >= early or d not in (0, depths - 1)] or left
            pick = min(allowed, key=lambda d: (use.get((step, d), 0), (d - me) % depths))
            use[step, pick] = use.get((step, pick), 0) + 1
            order.append(pick)
            left.remove(pick)
        orders.append(order + [me])
    return orders


def choose(index, values):
    out = jnp.int32(values[0])
    for i in range(1, len(values)):
        out = jnp.where(index == i, jnp.int32(values[i]), out)
    return out


def cell_terms(rate, centre, gx, gy, gz, state):
    run, light, total, skew, green = state
    facing = jnp.abs(gz + (LIGHT_X / LIGHT_Z) * gx + (LIGHT_Y / LIGHT_Z) * gy)
    norm = lax.rsqrt((gx * gx + 4.0) + (gy * gy + gz * gz))
    shade = facing * norm + 0.3 / SHADE
    squared = centre * centre
    run = run + squared * pltpu.reciprocal(1.0 + squared, approx=True)
    after = jnp.exp2(run * (-rate))
    weight = (light - after) * shade
    total = total + weight
    skew = skew + weight * jnp.tanh(centre)
    green = green + weight * jnp.exp2(squared * (-LOG2E))
    return run, after, total, skew, green


def render_kernel(
    tiles, depths, v_ref, o_ref, vin, ws, zout, zin, part, recv,
    load_sem, xs_sem, xr_sem, zs_sem, zr_sem, ps_sem, pr_sem,
):
    cx, cz, _ = v_ref.shape
    tile = lax.axis_index("tile")
    me = lax.axis_index("depth")
    tile_up, tile_down = lax.rem(tile + 1, tiles), lax.rem(tile + tiles - 1, tiles)
    deep_up, deep_down = lax.rem(me + 1, depths), lax.rem(me + depths - 1, depths)
    rate = OPACITY / (cz * depths) * LOG2E

    barrier = pltpu.get_barrier_semaphore()
    for other in (tile_up, tile_down):
        pl.semaphore_signal(barrier, inc=1, device_id={"tile": other}, device_id_type=MESH)
    for step in range(1, depths):
        pl.semaphore_signal(
            barrier, inc=1, device_id={"depth": lax.rem(me + step, depths)}, device_id_type=MESH
        )
    loads = []
    batch = cx // 4
    for i in range(4):
        loads.append(
            pltpu.make_async_copy(
                v_ref.at[pl.ds(i * batch, batch)], vin.at[pl.ds(1 + i * batch, batch)], load_sem.at[i]
            )
        )
        loads[-1].start()
    in_row = lax.broadcasted_iota(jnp.int32, (256, 256), 1)
    out_row = lax.broadcasted_iota(jnp.int32, (256, 256), 0)
    order = jnp.where(in_row == (out_row % 8) * 32 + out_row // 8, 1.0, 0.0).astype(jnp.bfloat16)
    lane = lax.broadcasted_iota(jnp.int32, (8, 128), 1)
    zeros = jnp.zeros((8, 128), jnp.float32)

    def clear(x, _):
        for h in range(2):
            for z in range(cz + 1):
                ws[x, h, pl.ds(LEAD + PITCH * z - 8, 8), :] = zeros
        return 0

    lax.fori_loop(0, cx + 2, clear, 0)

    pl.semaphore_wait(barrier, depths + 1)
    x_down = pltpu.make_async_remote_copy(
        v_ref.at[0], vin.at[cx + 1], xs_sem.at[0], xr_sem.at[0],
        device_id={"tile": tile_down}, device_id_type=MESH,
    )
    x_up = pltpu.make_async_remote_copy(
        v_ref.at[cx - 1], vin.at[0], xs_sem.at[1], xr_sem.at[1],
        device_id={"tile": tile_up}, device_id_type=MESH,
    )
    x_down.start()
    x_up.start()

    def relayout(x, keep=None):
        slab = vin[x]
        stacked = jnp.concatenate([slab[:, 256 * c : 256 * c + 256] for c in range(8)], axis=0)
        out = jnp.dot(order, stacked, preferred_element_type=jnp.float32)
        if keep is not None:
            out = out * keep
        for z in range(cz):
            for h in range(2):
                ws[x, h, pl.ds(LEAD + PITCH * z, 8), :] = out[8 * z : 8 * z + 8, 128 * h : 128 * h + 128]

    def own_slabs(i, _):
        relayout(1 + 2 * i)
        relayout(2 + 2 * i)
        return 0

    for i in range(4):
        loads[i].wait()
        lax.fori_loop(i * (batch // 2), (i + 1) * (batch // 2), own_slabs, 0)

    def cell(slab, z, h, shift=0):
        return ws[slab, h, pl.ds(LEAD + PITCH * z + shift, 8), :]

    def pack(x, _):
        for side, z in ((0, 0), (1, cz - 1)):
            rows = jnp.concatenate([cell(x + 1, z, 0), cell(x + 1, z, 1)], axis=0)
            zout[side, x] = rows.astype(jnp.bfloat16)
        return 0

    lax.fori_loop(0, cx, pack, 0)
    z_down = pltpu.make_async_remote_copy(
        zout.at[0], zin.at[1], zs_sem.at[0], zr_sem.at[0],
        device_id={"depth": deep_down}, device_id_type=MESH,
    )
    z_up = pltpu.make_async_remote_copy(
        zout.at[1], zin.at[0], zs_sem.at[1], zr_sem.at[1],
        device_id={"depth": deep_up}, device_id_type=MESH,
    )
    z_down.start()
    z_up.start()

    def y_differences(slab, z):
        first, second = cell(slab, z, 0), cell(slab, z, 1)
        above, below = cell(slab, z, 0, 1), cell(slab, z, 1, -1)
        right_0 = pltpu.roll(jnp.where(lane == 0, second, first), 127, 1)
        right_1 = pltpu.roll(jnp.where(lane == 0, above, second), 127, 1)
        left_0 = pltpu.roll(jnp.where(lane == 127, below, first), 1, 1)
        left_1 = pltpu.roll(jnp.where(lane == 127, first, second), 1, 1)
        return right_0 - left_0, right_1 - left_1

    def inner(d):
        def column(x, _):
            slab = 2 * d + x + 1
            state = []
            for h in range(2):
                squared = cell(slab, 0, h) ** 2
                run = squared * pltpu.reciprocal(1.0 + squared, approx=True)
                state.append((run, jnp.exp2(run * (-rate)), zeros, zeros, zeros))
            for z in range(1, cz - 1):
                gy = y_differences(slab, z)
                for h in range(2):
                    state[h] = cell_terms(
                        rate,
                        cell(slab, z, h),
                        cell(slab + 1, z, h) - cell(slab - 1, z, h),
                        gy[h],
                        cell(slab, z + 1, h) - cell(slab, z - 1, h),
                        state[h],
                    )
            for h in range(2):
                run, _, total, skew, green = state[h]
                for channel, value in enumerate((total, skew, green, run)):
                    part[d, channel, x, h] = value
            return 0

        lax.fori_loop(0, 2, column, 0)

    near = jnp.where(me == 0, 0.0, 1.0)
    far = jnp.where(me == depths - 1, 0.0, 1.0)

    def outer(d):
        for x in range(2):
            slab = 2 * d + x + 1
            front = zin[0, slab - 1].astype(jnp.float32) * near
            back = zin[1, slab - 1].astype(jnp.float32) * far
            gy_first, gy_last = y_differences(slab, 0), y_differences(slab, cz - 1)
            for h in range(2):
                total, skew, green, run = (part[d, channel, x, h] for channel in range(4))
                _, _, total, skew, green = cell_terms(
                    rate,
                    cell(slab, 0, h),
                    cell(slab + 1, 0, h) - cell(slab - 1, 0, h),
                    gy_first[h],
                    cell(slab, 1, h) - front[8 * h : 8 * h + 8],
                    (zeros, 1.0, total, skew, green),
                )
                run, _, total, skew, green = cell_terms(
                    rate,
                    cell(slab, cz - 1, h),
                    cell(slab + 1, cz - 1, h) - cell(slab - 1, cz - 1, h),
                    gy_last[h],
                    back[8 * h : 8 * h + 8] - cell(slab, cz - 2, h),
                    (run, jnp.exp2(run * (-rate)), total, skew, green),
                )
                for channel, value in enumerate((total, skew, green, run)):
                    part[d, channel, x, h] = value

    def send(d):
        return pltpu.make_async_remote_copy(
            part.at[d], recv.at[me], ps_sem.at[d], pr_sem.at[me],
            device_id={"depth": d}, device_id_type=MESH,
        )

    codes = []
    orders = plan(depths)
    for s in range(depths):
        codes.append(sum(orders[k][s] * depths**k for k in range(depths)))
    power = choose(me, [depths**k for k in range(depths)])

    def target(s):
        return lax.rem(choose(s, codes) // power, depths)

    def finish(s, _):
        d = target(s)
        outer(d)

        @pl.when(s < depths - 1)
        def _():
            send(d).start()

        return 0

    def step(s, _):
        inner(target(s))

        @pl.when(s == 1)
        def _():
            z_down.wait_recv()
            z_up.wait_recv()

        @pl.when(s == EARLY - 1)
        def _():
            x_down.wait_recv()
            x_up.wait_recv()
            relayout(0, jnp.where(tile == 0, 0.0, 1.0))
            relayout(cx + 1, jnp.where(tile == tiles - 1, 0.0, 1.0))

        @pl.when(s >= 1)
        def _():
            lax.fori_loop(jnp.where(s == 1, 0, s), s + 1, finish, 0)

        return 0

    lax.fori_loop(0, depths, step, 0)
    recv[me] = part[me]

    for s in range(1, depths):
        source = lax.rem(me + s, depths)
        pltpu.make_async_remote_copy(
            part.at[source], recv.at[source], ps_sem.at[source], pr_sem.at[source],
            device_id={"depth": source}, device_id_type=MESH,
        ).wait_recv()

    half = 0.5 * SHADE
    for h in range(2):
        done = []
        for x in range(2):
            total, skew, green, run = (recv[0, channel, x, h] for channel in range(4))
            for k in range(1, depths):
                light = jnp.exp2(run * (-rate))
                total = total + light * recv[k, 0, x, h]
                skew = skew + light * recv[k, 1, x, h]
                green = green + light * recv[k, 2, x, h]
                run = run + recv[k, 3, x, h]
            done.append(
                (half * (total + skew), half * green, half * (total - skew), 1.0 - jnp.exp2(run * (-rate)))
            )
        for channel in range(4):
            for c in range(8):
                rows = [done[x][channel][c : c + 1] for x in range(2)]
                o_ref[channel, :, 256 * c + 128 * h : 256 * c + 128 * h + 128] = jnp.concatenate(rows, axis=0)

    x_down.wait_send()
    x_up.wait_send()
    z_down.wait_send()
    z_up.wait_send()
    for s in range(1, depths):
        send(lax.rem(me + s, depths)).wait_send()


def shards(volume):
    tiles, depths = lax.axis_size("tile"), lax.axis_size("depth")
    cx, cz, ny = volume.shape
    dma = pltpu.SemaphoreType.DMA
    return pl.pallas_call(
        functools.partial(render_kernel, tiles, depths),
        out_shape=jax.ShapeDtypeStruct((4, cx // depths, ny), jnp.float32),
        in_specs=[pl.BlockSpec(memory_space=pltpu.HBM)],
        out_specs=pl.BlockSpec(memory_space=pltpu.VMEM),
        scratch_shapes=[
            pltpu.VMEM((cx + 2, cz, ny), jnp.bfloat16),
            pltpu.VMEM((cx + 2, 2, LEAD + PITCH * cz, 128), jnp.float32),
            pltpu.VMEM((2, cx, 16, 128), jnp.bfloat16),
            pltpu.VMEM((2, cx, 16, 128), jnp.bfloat16),
            pltpu.VMEM((depths, 4, 2, 2, 8, 128), jnp.float32),
            pltpu.VMEM((depths, 4, 2, 2, 8, 128), jnp.float32),
            dma((4,)), dma((2,)), dma((2,)), dma((2,)), dma((2,)), dma((depths,)), dma((depths,)),
        ],
        compiler_params=pltpu.CompilerParams(
            collective_id=0, has_side_effects=True, vmem_limit_bytes=61 * 1024 * 1024
        ),
        cost_estimate=pl.CostEstimate(flops=50_000_000, bytes_accessed=2_300_000, transcendentals=5_000_000),
    )(volume)


def solution(mesh):
    in_specs = (P("tile", "depth", None),)
    out_specs = P(None, ("tile", "depth"), None)
    return jax.shard_map(shards, mesh=mesh, in_specs=in_specs, out_specs=out_specs, check_vma=False)
```

time: 41.6 us -> 38.6 us (0.928)
  Pallas kernels: 39.9 us -> 36.9 us
    pallas_call x1, Pallas kernels: 39.9 us -> 36.9 us  [shards(): pl.pallas_call(functools.partial(render_kernel, tiles, depths), out_shape...]
    reshape x1 -> x0, local copies, waits for them, and re-layouts: 1.51 us -> none  [shards(): return image.reshape(4, cx // depths, ny)]
    unnamed x0 -> x1, local copies, waits for them, and re-layouts: none -> 1.47 us
where the time goes in v2:
time: 38.6 us; the launch traced here: 38.4 us
  Pallas kernels  36.9 us (96%)
  local copies, waits for them, and re-layouts  1.47 us (4%)
    pallas_call x1, Pallas kernels, shards(): pl.pallas_call(functools.partial(render_kernel, tiles, depths), out_shape...  36.9 us
    unnamed x1, local copies, waits for them, and re-layouts  1.47 us

profile of v2, /device:TPU:1, one launch (start us, length us, event | category | flops | bytes accessed | tf_op | source)
XLA Modules:
  0.0 38.4 jit_solution(10380663152291867779)
XLA Ops:
  0.0 36.9 %shard_map.17 = f32[4,2,2048]{2,1,0:T(2,128)} custom-call(bf16[16,32,2048]{2,1,0:T(8,128)(2,1)} %v_ref.1), custom_call_target="tpu_custom_call" | custom-call | flops 50000000 | bytes 2300000 | tf_op jit(solution)/shard_map/pallas_call | solution.py:308
  36.9 1.5 %copy.3 = f32[4,2,2048]{2,1,0:T(2,128)} copy(f32[4,2,2048]{2,1,0:T(2,128)} %shard_map.17) | data formatting | bytes 131072

commit v3 on v2

--- a/solution.py
+++ b/solution.py
@@ -16,20 +16,29 @@
 SHADE = 0.7 * LIGHT_Z
 PITCH = 16
 LEAD = 8
-EARLY = 3
+EARLY = 4
+FIRST = 3
+POWER = 12
+SCALES = (256.0, 512.0, 256.0, 32.0)
 MESH = pl.DeviceIdType.MESH
 
 
 def plan(depths):
-    early = min(EARLY, depths - 2)
     use = {}
     orders = []
+    chips = depths // 2
     for me in range(depths):
-        left = [(me + s) % depths for s in range(1, depths)]
+
+        def hops(d):
+            apart = abs(d // 2 - me // 2)
+            return min(apart, chips - apart)
+
+        left = [d for d in range(depths) if d != me]
         order = []
         for step in range(depths - 1):
-            allowed = [d for d in left if step >= early or d not in (0, depths - 1)] or left
-            pick = min(allowed, key=lambda d: (use.get((step, d), 0), (d - me) % depths))
+            allowed = [d for d in left if hops(d) > 0 or len(left) == 1]
+            allowed = [d for d in allowed if step >= EARLY or d not in (0, depths - 1)] or left
+            pick = min(allowed, key=lambda d: (use.get((step, d), 0) - hops(d), (d - me) % depths))
             use[step, pick] = use.get((step, pick), 0) + 1
             order.append(pick)
             left.remove(pick)
@@ -42,6 +51,16 @@
     for i in range(1, len(values)):
         out = jnp.where(index == i, jnp.int32(values[i]), out)
     return out
+
+
+def encode(value, scale):
+    value = value * scale
+    fourth = (value * value) * (value * value)
+    return fourth * fourth * fourth
+
+
+def decode(code, scale):
+    return jnp.exp2(jnp.log2(code.astype(jnp.float32)) * (1.0 / POWER) - math.log2(scale))
 
 
 def cell_terms(rate, centre, gx, gy, gz, state):
@@ -60,7 +79,7 @@
 
 
 def render_kernel(
-    tiles, depths, v_ref, o_ref, vin, ws, zout, zin, part, recv,
+    tiles, depths, v_ref, o_ref, vin, ws, zout, zin, part, coded, recv,
     load_sem, xs_sem, xr_sem, zs_sem, zr_sem, ps_sem, pr_sem,
 ):
     cx, cz, _ = v_ref.shape
@@ -100,7 +119,6 @@
 
     lax.fori_loop(0, cx + 2, clear, 0)
 
-    pl.semaphore_wait(barrier, depths + 1)
     x_down = pltpu.make_async_remote_copy(
         v_ref.at[0], vin.at[cx + 1], xs_sem.at[0], xr_sem.at[0],
         device_id={"tile": tile_down}, device_id_type=MESH,
@@ -109,9 +127,6 @@
         v_ref.at[cx - 1], vin.at[0], xs_sem.at[1], xr_sem.at[1],
         device_id={"tile": tile_up}, device_id_type=MESH,
     )
-    x_down.start()
-    x_up.start()
-
     def relayout(x, keep=None):
         slab = vin[x]
         stacked = jnp.concatenate([slab[:, 256 * c : 256 * c + 256] for c in range(8)], axis=0)
@@ -122,14 +137,17 @@
             for h in range(2):
                 ws[x, h, pl.ds(LEAD + PITCH * z, 8), :] = out[8 * z : 8 * z + 8, 128 * h : 128 * h + 128]
 
-    def own_slabs(i, _):
-        relayout(1 + 2 * i)
-        relayout(2 + 2 * i)
-        return 0
+    def own_slabs(i):
+        for x in range(batch):
+            relayout(1 + batch * i + x)
 
     for i in range(4):
         loads[i].wait()
-        lax.fori_loop(i * (batch // 2), (i + 1) * (batch // 2), own_slabs, 0)
+        own_slabs(i)
+        if i == 1:
+            pl.semaphore_wait(barrier, depths + 1)
+            x_down.start()
+            x_up.start()
 
     def cell(slab, z, h, shift=0):
         return ws[slab, h, pl.ds(LEAD + PITCH * z + shift, 8), :]
@@ -215,12 +233,15 @@
                     back[8 * h : 8 * h + 8] - cell(slab, cz - 2, h),
                     (run, jnp.exp2(run * (-rate)), total, skew, green),
                 )
-                for channel, value in enumerate((total, skew, green, run)):
+                for channel, value in enumerate((total + skew, green, total - skew, run)):
                     part[d, channel, x, h] = value
+            for channel in range(4):
+                rows = [encode(part[d, channel, x, h], SCALES[channel]) for h in range(2)]
+                coded[d, channel, x] = jnp.concatenate(rows, axis=0).astype(jnp.bfloat16)
 
     def send(d):
         return pltpu.make_async_remote_copy(
-            part.at[d], recv.at[me], ps_sem.at[d], pr_sem.at[me],
+            coded.at[d], recv.at[me], ps_sem.at[d], pr_sem.at[me],
             device_id={"depth": d}, device_id_type=MESH,
         )
 
@@ -246,7 +267,7 @@
     def step(s, _):
         inner(target(s))
 
-        @pl.when(s == 1)
+        @pl.when(s == FIRST - 1)
         def _():
             z_down.wait_recv()
             z_up.wait_recv()
@@ -258,40 +279,36 @@
             relayout(0, jnp.where(tile == 0, 0.0, 1.0))
             relayout(cx + 1, jnp.where(tile == tiles - 1, 0.0, 1.0))
 
-        @pl.when(s >= 1)
+        @pl.when(s >= FIRST - 1)
         def _():
-            lax.fori_loop(jnp.where(s == 1, 0, s), s + 1, finish, 0)
+            lax.fori_loop(jnp.where(s == FIRST - 1, 0, s), s + 1, finish, 0)
 
         return 0
 
     lax.fori_loop(0, depths, step, 0)
-    recv[me] = part[me]
+    recv[me] = coded[me]
 
     for s in range(1, depths):
         source = lax.rem(me + s, depths)
         pltpu.make_async_remote_copy(
-            part.at[source], recv.at[source], ps_sem.at[source], pr_sem.at[source],
+            coded.at[source], recv.at[source], ps_sem.at[source], pr_sem.at[source],
             device_id={"depth": source}, device_id_type=MESH,
         ).wait_recv()
 
-    half = 0.5 * SHADE
-    for h in range(2):
-        done = []
-        for x in range(2):
-            total, skew, green, run = (recv[0, channel, x, h] for channel in range(4))
-            for k in range(1, depths):
-                light = jnp.exp2(run * (-rate))
-                total = total + light * recv[k, 0, x, h]
-                skew = skew + light * recv[k, 1, x, h]
-                green = green + light * recv[k, 2, x, h]
-                run = run + recv[k, 3, x, h]
-            done.append(
-                (half * (total + skew), half * green, half * (total - skew), 1.0 - jnp.exp2(run * (-rate)))
-            )
+    for x in range(2):
+        run = jnp.zeros((16, 128), jnp.float32)
+        colours = [run, run, run]
+        for k in range(depths):
+            light = jnp.exp2(run * (-rate))
+            for channel in range(3):
+                colours[channel] += light * decode(recv[k, channel, x], SCALES[channel])
+            run = run + decode(recv[k, 3, x], SCALES[3])
+        image = [0.5 * SHADE * colour for colour in colours] + [1.0 - jnp.exp2(run * (-rate))]
         for channel in range(4):
-            for c in range(8):
-                rows = [done[x][channel][c : c + 1] for x in range(2)]
-                o_ref[channel, :, 256 * c + 128 * h : 256 * c + 128 * h + 128] = jnp.concatenate(rows, axis=0)
+            for h in range(2):
+                for c in range(8):
+                    y = 256 * c + 128 * h
+                    o_ref[channel, x : x + 1, y : y + 128] = image[channel][8 * h + c : 8 * h + c + 1]
 
     x_down.wait_send()
     x_up.wait_send()
@@ -316,11 +333,12 @@
             pltpu.VMEM((2, cx, 16, 128), jnp.bfloat16),
             pltpu.VMEM((2, cx, 16, 128), jnp.bfloat16),
             pltpu.VMEM((depths, 4, 2, 2, 8, 128), jnp.float32),
-            pltpu.VMEM((depths, 4, 2, 2, 8, 128), jnp.float32),
+            pltpu.VMEM((depths, 4, 2, 16, 128), jnp.bfloat16),
+            pltpu.VMEM((depths, 4, 2, 16, 128), jnp.bfloat16),
             dma((4,)), dma((2,)), dma((2,)), dma((2,)), dma((2,)), dma((depths,)), dma((depths,)),
         ],
         compiler_params=pltpu.CompilerParams(
-            collective_id=0, has_side_effects=True, vmem_limit_bytes=61 * 1024 * 1024
+            collective_id=0, has_side_effects=True, vmem_limit_bytes=52 * 1024 * 1024
         ),
         cost_estimate=pl.CostEstimate(flops=50_000_000, bytes_accessed=2_300_000, transcendentals=5_000_000),
     )(volume)

time: 38.6 us -> 33.2 us (0.86)
  Pallas kernels: 36.9 us -> 32.4 us
  local copies, waits for them, and re-layouts: 1.47 us -> 0.63 us
    pallas_call x1, Pallas kernels: 36.9 us -> 32.4 us  [shards(): pl.pallas_call(functools.partial(render_kernel, tiles, depths), out_shape...]
    unnamed x1, local copies, waits for them, and re-layouts: 1.47 us -> 0.63 us
where the time goes in v3:
time: 33.2 us; the launch traced here: 33 us
  Pallas kernels  32.4 us (98%)
  local copies, waits for them, and re-layouts  0.63 us (2%)
    pallas_call x1, Pallas kernels, shards(): pl.pallas_call(functools.partial(render_kernel, tiles, depths), out_shape...  32.4 us

profile of v3, /device:TPU:1, one launch (start us, length us, event | category | flops | bytes accessed | tf_op | source)
XLA Modules:
  0.0 33.0 jit_solution(2800788115401917587)
XLA Ops:
  0.0 32.4 %shard_map.17 = f32[4,2,2048]{2,1,0:T(2,128)S(1)} custom-call(bf16[16,32,2048]{2,1,0:T(8,128)(2,1)} %v_ref.1), custom_call_target="tpu_custom_call" | custom-call | flops 50000000 | bytes 2300000 | tf_op jit(solution)/shard_map/pallas_call | solution.py:325
  32.4 0.6 %copy.3 = f32[4,2,2048]{2,1,0:T(2,128)} copy(f32[4,2,2048]{2,1,0:T(2,128)S(1)} %shard_map.17) | data formatting | bytes 131072

commit v4 on v3

--- a/solution.py
+++ b/solution.py
@@ -16,7 +16,7 @@
 SHADE = 0.7 * LIGHT_Z
 PITCH = 16
 LEAD = 8
-EARLY = 4
+EARLY = 5
 FIRST = 3
 POWER = 12
 SCALES = (256.0, 512.0, 256.0, 32.0)
@@ -36,8 +36,8 @@
         left = [d for d in range(depths) if d != me]
         order = []
         for step in range(depths - 1):
-            allowed = [d for d in left if hops(d) > 0 or len(left) == 1]
-            allowed = [d for d in allowed if step >= EARLY or d not in (0, depths - 1)] or left
+            allowed = [d for d in left if step >= EARLY or d not in (0, depths - 1)]
+            allowed = [d for d in allowed if hops(d) > 0] or allowed
             pick = min(allowed, key=lambda d: (use.get((step, d), 0) - hops(d), (d - me) % depths))
             use[step, pick] = use.get((step, pick), 0) + 1
             order.append(pick)
@@ -65,8 +65,8 @@
 
 def cell_terms(rate, centre, gx, gy, gz, state):
     run, light, total, skew, green = state
-    facing = jnp.abs(gz + (LIGHT_X / LIGHT_Z) * gx + (LIGHT_Y / LIGHT_Z) * gy)
-    norm = lax.rsqrt((gx * gx + 4.0) + (gy * gy + gz * gz))
+    facing = jnp.abs((gz + (LIGHT_X / LIGHT_Z) * gx) + (LIGHT_Y / LIGHT_Z) * gy)
+    norm = lax.rsqrt(((gx * gx + 4.0) + gz * gz) + gy * gy)
     shade = facing * norm + 0.3 / SHADE
     squared = centre * centre
     run = run + squared * pltpu.reciprocal(1.0 + squared, approx=True)
@@ -86,12 +86,17 @@
     tile = lax.axis_index("tile")
     me = lax.axis_index("depth")
     tile_up, tile_down = lax.rem(tile + 1, tiles), lax.rem(tile + tiles - 1, tiles)
+    has_up, has_down = tile < tiles - 1, tile > 0
     deep_up, deep_down = lax.rem(me + 1, depths), lax.rem(me + depths - 1, depths)
     rate = OPACITY / (cz * depths) * LOG2E
 
     barrier = pltpu.get_barrier_semaphore()
-    for other in (tile_up, tile_down):
-        pl.semaphore_signal(barrier, inc=1, device_id={"tile": other}, device_id_type=MESH)
+    for other, there in ((tile_up, has_up), (tile_down, has_down)):
+
+        @pl.when(there)
+        def _():
+            pl.semaphore_signal(barrier, inc=1, device_id={"tile": other}, device_id_type=MESH)
+
     for step in range(1, depths):
         pl.semaphore_signal(
             barrier, inc=1, device_id={"depth": lax.rem(me + step, depths)}, device_id_type=MESH
@@ -118,6 +123,14 @@
         return 0
 
     lax.fori_loop(0, cx + 2, clear, 0)
+    for x, there in ((0, has_down), (cx + 1, has_up)):
+
+        @pl.when(jnp.logical_not(there))
+        def _():
+            for h in range(2):
+                for z in range(cz):
+                    ws[x, h, pl.ds(LEAD + PITCH * z, 8), :] = zeros
+
 
     x_down = pltpu.make_async_remote_copy(
         v_ref.at[0], vin.at[cx + 1], xs_sem.at[0], xr_sem.at[0],
@@ -127,12 +140,10 @@
         v_ref.at[cx - 1], vin.at[0], xs_sem.at[1], xr_sem.at[1],
         device_id={"tile": tile_up}, device_id_type=MESH,
     )
-    def relayout(x, keep=None):
+    def relayout(x):
         slab = vin[x]
         stacked = jnp.concatenate([slab[:, 256 * c : 256 * c + 256] for c in range(8)], axis=0)
         out = jnp.dot(order, stacked, preferred_element_type=jnp.float32)
-        if keep is not None:
-            out = out * keep
         for z in range(cz):
             for h in range(2):
                 ws[x, h, pl.ds(LEAD + PITCH * z, 8), :] = out[8 * z : 8 * z + 8, 128 * h : 128 * h + 128]
@@ -145,9 +156,9 @@
         loads[i].wait()
         own_slabs(i)
         if i == 1:
-            pl.semaphore_wait(barrier, depths + 1)
-            x_down.start()
-            x_up.start()
+            pl.semaphore_wait(barrier, depths - 1 + jnp.where(has_up, 1, 0) + jnp.where(has_down, 1, 0))
+            pl.when(has_down)(x_down.start)
+            pl.when(has_up)(x_up.start)
 
     def cell(slab, z, h, shift=0):
         return ws[slab, h, pl.ds(LEAD + PITCH * z + shift, 8), :]
@@ -179,6 +190,48 @@
         left_1 = pltpu.roll(jnp.where(lane == 127, first, second), 1, 1)
         return right_0 - left_0, right_1 - left_1
 
+    near = jnp.where(me == 0, 0.0, 1.0)
+    far = jnp.where(me == depths - 1, 0.0, 1.0)
+
+    def x_difference(slab, z, h):
+        return cell(slab + 1, z, h) - cell(slab - 1, z, h)
+
+    def front_layer(slab, state):
+        halo = zin[0, slab - 1].astype(jnp.float32) * near
+        gy = y_differences(slab, 0)
+        out = []
+        for h in range(2):
+            gz = cell(slab, 1, h) - halo[8 * h : 8 * h + 8]
+            out.append(cell_terms(rate, cell(slab, 0, h), x_difference(slab, 0, h), gy[h], gz, state[h]))
+        return out
+
+    def back_layer(slab, state):
+        halo = zin[1, slab - 1].astype(jnp.float32) * far
+        gy = y_differences(slab, cz - 1)
+        out = []
+        for h in range(2):
+            gz = halo[8 * h : 8 * h + 8] - cell(slab, cz - 2, h)
+            out.append(
+                cell_terms(rate, cell(slab, cz - 1, h), x_difference(slab, cz - 1, h), gy[h], gz, state[h])
+            )
+        return out
+
+    def inner_layers(slab, state):
+        for z in range(1, cz - 1):
+            gy = y_differences(slab, z)
+            for h in range(2):
+                gz = cell(slab, z + 1, h) - cell(slab, z - 1, h)
+                state[h] = cell_terms(rate, cell(slab, z, h), x_difference(slab, z, h), gy[h], gz, state[h])
+        return state
+
+    def store(d, x, state):
+        pairs = []
+        for run, _, total, skew, green in state:
+            pairs.append([encode(v, s) for v, s in zip((total + skew, green, total - skew, run), SCALES)])
+        for channel in range(4):
+            rows = jnp.concatenate([pairs[0][channel], pairs[1][channel]], axis=0)
+            coded[d, channel, x] = rows.astype(jnp.bfloat16)
+
     def inner(d):
         def column(x, _):
             slab = 2 * d + x + 1
@@ -187,17 +240,7 @@
                 squared = cell(slab, 0, h) ** 2
                 run = squared * pltpu.reciprocal(1.0 + squared, approx=True)
                 state.append((run, jnp.exp2(run * (-rate)), zeros, zeros, zeros))
-            for z in range(1, cz - 1):
-                gy = y_differences(slab, z)
-                for h in range(2):
-                    state[h] = cell_terms(
-                        rate,
-                        cell(slab, z, h),
-                        cell(slab + 1, z, h) - cell(slab - 1, z, h),
-                        gy[h],
-                        cell(slab, z + 1, h) - cell(slab, z - 1, h),
-                        state[h],
-                    )
+            state = inner_layers(slab, state)
             for h in range(2):
                 run, _, total, skew, green = state[h]
                 for channel, value in enumerate((total, skew, green, run)):
@@ -206,38 +249,28 @@
 
         lax.fori_loop(0, 2, column, 0)
 
-    near = jnp.where(me == 0, 0.0, 1.0)
-    far = jnp.where(me == depths - 1, 0.0, 1.0)
-
     def outer(d):
         for x in range(2):
             slab = 2 * d + x + 1
-            front = zin[0, slab - 1].astype(jnp.float32) * near
-            back = zin[1, slab - 1].astype(jnp.float32) * far
-            gy_first, gy_last = y_differences(slab, 0), y_differences(slab, cz - 1)
+            state = []
             for h in range(2):
                 total, skew, green, run = (part[d, channel, x, h] for channel in range(4))
-                _, _, total, skew, green = cell_terms(
-                    rate,
-                    cell(slab, 0, h),
-                    cell(slab + 1, 0, h) - cell(slab - 1, 0, h),
-                    gy_first[h],
-                    cell(slab, 1, h) - front[8 * h : 8 * h + 8],
-                    (zeros, 1.0, total, skew, green),
-                )
-                run, _, total, skew, green = cell_terms(
-                    rate,
-                    cell(slab, cz - 1, h),
-                    cell(slab + 1, cz - 1, h) - cell(slab - 1, cz - 1, h),
-                    gy_last[h],
-                    back[8 * h : 8 * h + 8] - cell(slab, cz - 2, h),
-                    (run, jnp.exp2(run * (-rate)), total, skew, green),
-                )
-                for channel, value in enumerate((total + skew, green, total - skew, run)):
-                    part[d, channel, x, h] = value
-            for channel in range(4):
-                rows = [encode(part[d, channel, x, h], SCALES[channel]) for h in range(2)]
-                coded[d, channel, x] = jnp.concatenate(rows, axis=0).astype(jnp.bfloat16)
+                state.append((zeros, 1.0, total, skew, green))
+            done = front_layer(slab, state)
+            state = []
+            for h in range(2):
+                run = part[d, 3, x, h]
+                state.append((run, jnp.exp2(run * (-rate)), *done[h][2:]))
+            store(d, x, back_layer(slab, state))
+
+    def whole(d):
+        def column(x, _):
+            slab = 2 * d + x + 1
+            state = front_layer(slab, [(zeros, 1.0, zeros, zeros, zeros)] * 2)
+            store(d, x, back_layer(slab, inner_layers(slab, state)))
+            return 0
+
+        lax.fori_loop(0, 2, column, 0)
 
     def send(d):
         return pltpu.make_async_remote_copy(
@@ -254,9 +287,32 @@
     def target(s):
         return lax.rem(choose(s, codes) // power, depths)
 
-    def finish(s, _):
+    def early(s, _):
+        inner(target(s))
+        return 0
+
+    def early_end(s, _):
         d = target(s)
         outer(d)
+        send(d).start()
+        return 0
+
+    def late(s, _):
+        @pl.when(s == EARLY)
+        def _():
+            @pl.when(has_down)
+            def _():
+                x_up.wait_recv()
+                relayout(0)
+
+            @pl.when(has_up)
+            def _():
+                x_down.wait_recv()
+                relayout(cx + 1)
+
+
+        d = target(s)
+        whole(d)
 
         @pl.when(s < depths - 1)
         def _():
@@ -264,28 +320,11 @@
 
         return 0
 
-    def step(s, _):
-        inner(target(s))
-
-        @pl.when(s == FIRST - 1)
-        def _():
-            z_down.wait_recv()
-            z_up.wait_recv()
-
-        @pl.when(s == EARLY - 1)
-        def _():
-            x_down.wait_recv()
-            x_up.wait_recv()
-            relayout(0, jnp.where(tile == 0, 0.0, 1.0))
-            relayout(cx + 1, jnp.where(tile == tiles - 1, 0.0, 1.0))
-
-        @pl.when(s >= FIRST - 1)
-        def _():
-            lax.fori_loop(jnp.where(s == FIRST - 1, 0, s), s + 1, finish, 0)
-
-        return 0
-
-    lax.fori_loop(0, depths, step, 0)
+    lax.fori_loop(0, FIRST, early, 0)
+    z_down.wait_recv()
+    z_up.wait_recv()
+    lax.fori_loop(0, FIRST, early_end, 0)
+    lax.fori_loop(FIRST, depths, late, 0)
     recv[me] = coded[me]
 
     for s in range(1, depths):
@@ -310,8 +349,8 @@
                     y = 256 * c + 128 * h
                     o_ref[channel, x : x + 1, y : y + 128] = image[channel][8 * h + c : 8 * h + c + 1]
 
-    x_down.wait_send()
-    x_up.wait_send()
+    pl.when(has_down)(x_down.wait_send)
+    pl.when(has_up)(x_up.wait_send)
     z_down.wait_send()
     z_up.wait_send()
     for s in range(1, depths):

time: 33.2 us -> 31 us (0.934)
  the two profiles are of different devices: /device:TPU:1 before, /device:TPU:56 now
where the time goes in v4:
time: 31 us; the launch traced here: 30.8 us
  Pallas kernels  30.2 us (97%)
  local copies, waits for them, and re-layouts  0.63 us (2%)
    pallas_call x1, Pallas kernels, shards(): pl.pallas_call(functools.partial(render_kernel, tiles, depths), out_shape...  30.2 us
    unnamed x1, local copies, waits for them, and re-layouts  0.63 us

profile of v4, /device:TPU:56, one launch (start us, length us, event | category | flops | bytes accessed | tf_op | source)
XLA Modules:
  0.0 30.8 jit_solution(2333422467268272332)
XLA Ops:
  0.0 30.2 %shard_map.17 = f32[4,2,2048]{2,1,0:T(2,128)S(1)} custom-call(bf16[16,32,2048]{2,1,0:T(8,128)(2,1)} %v_ref.1), custom_call_target="tpu_custom_call" | custom-call | flops 50000000 | bytes 2300000 | tf_op jit(solution)/shard_map/pallas_call | solution.py:364
  30.2 0.6 %copy.3 = f32[4,2,2048]{2,1,0:T(2,128)} copy(f32[4,2,2048]{2,1,0:T(2,128)S(1)} %shard_map.17) | data formatting | bytes 131072

commit v5 on v4

--- a/solution.py
+++ b/solution.py
@@ -16,41 +16,12 @@
 SHADE = 0.7 * LIGHT_Z
 PITCH = 16
 LEAD = 8
-EARLY = 5
-FIRST = 3
+FIRST = 8
+FAR = 4
+EDGE = 12
 POWER = 12
 SCALES = (256.0, 512.0, 256.0, 32.0)
 MESH = pl.DeviceIdType.MESH
-
-
-def plan(depths):
-    use = {}
-    orders = []
-    chips = depths // 2
-    for me in range(depths):
-
-        def hops(d):
-            apart = abs(d // 2 - me // 2)
-            return min(apart, chips - apart)
-
-        left = [d for d in range(depths) if d != me]
-        order = []
-        for step in range(depths - 1):
-            allowed = [d for d in left if step >= EARLY or d not in (0, depths - 1)]
-            allowed = [d for d in allowed if hops(d) > 0] or allowed
-            pick = min(allowed, key=lambda d: (use.get((step, d), 0) - hops(d), (d - me) % depths))
-            use[step, pick] = use.get((step, pick), 0) + 1
-            order.append(pick)
-            left.remove(pick)
-        orders.append(order + [me])
-    return orders
-
-
-def choose(index, values):
-    out = jnp.int32(values[0])
-    for i in range(1, len(values)):
-        out = jnp.where(index == i, jnp.int32(values[i]), out)
-    return out
 
 
 def encode(value, scale):
@@ -90,6 +61,16 @@
     deep_up, deep_down = lax.rem(me + 1, depths), lax.rem(me + depths - 1, depths)
     rate = OPACITY / (cz * depths) * LOG2E
 
+    batch = cx // 4
+
+    def load(i):
+        return pltpu.make_async_copy(
+            v_ref.at[pl.ds(i * batch, batch)], vin.at[pl.ds(1 + i * batch, batch)], load_sem.at[i]
+        )
+
+    for i in range(4):
+        load(i).start()
+
     barrier = pltpu.get_barrier_semaphore()
     for other, there in ((tile_up, has_up), (tile_down, has_down)):
 
@@ -101,15 +82,6 @@
         pl.semaphore_signal(
             barrier, inc=1, device_id={"depth": lax.rem(me + step, depths)}, device_id_type=MESH
         )
-    loads = []
-    batch = cx // 4
-    for i in range(4):
-        loads.append(
-            pltpu.make_async_copy(
-                v_ref.at[pl.ds(i * batch, batch)], vin.at[pl.ds(1 + i * batch, batch)], load_sem.at[i]
-            )
-        )
-        loads[-1].start()
     in_row = lax.broadcasted_iota(jnp.int32, (256, 256), 1)
     out_row = lax.broadcasted_iota(jnp.int32, (256, 256), 0)
     order = jnp.where(in_row == (out_row % 8) * 32 + out_row // 8, 1.0, 0.0).astype(jnp.bfloat16)
@@ -148,17 +120,20 @@
             for h in range(2):
                 ws[x, h, pl.ds(LEAD + PITCH * z, 8), :] = out[8 * z : 8 * z + 8, 128 * h : 128 * h + 128]
 
-    def own_slabs(i):
+    def own_slabs(i, _):
+        load(i).wait()
         for x in range(batch):
             relayout(1 + batch * i + x)
 
-    for i in range(4):
-        loads[i].wait()
-        own_slabs(i)
-        if i == 1:
+        @pl.when(i == 2)
+        def _():
             pl.semaphore_wait(barrier, depths - 1 + jnp.where(has_up, 1, 0) + jnp.where(has_down, 1, 0))
             pl.when(has_down)(x_down.start)
             pl.when(has_up)(x_up.start)
+
+        return 0
+
+    lax.fori_loop(0, cx // batch, own_slabs, 0)
 
     def cell(slab, z, h, shift=0):
         return ws[slab, h, pl.ds(LEAD + PITCH * z + shift, 8), :]
@@ -224,81 +199,72 @@
                 state[h] = cell_terms(rate, cell(slab, z, h), x_difference(slab, z, h), gy[h], gz, state[h])
         return state
 
-    def store(d, x, state):
+    width = 2 * depths
+    first, last = me == 0, me == depths - 1
+    edges = jnp.where(first | last, 1, 2)
+    count = width - 2 - edges
+    start = jnp.where(last, 0, 2 * me + 1)
+    edge = jnp.where(last | ((lax.rem(me, 2) == 0) & jnp.logical_not(first)), 0, width - 1)
+    own = jnp.where(first, 1, 2 * me)
+
+    def target(p):
+        turn = jnp.where(p < EDGE, p, p - edges) + FAR
+        turn = jnp.where(turn >= count, turn - count, turn)
+        inside = start + turn
+        inside = jnp.where(inside >= width - 2, inside - (width - 2), inside) + 1
+        middle = jnp.where(p == EDGE, edge, width - 1 - edge)
+        late = jnp.where(p == width - 2, own, 4 * me + 1 - own)
+        at_edge = (p >= EDGE) & (p < EDGE + edges)
+        return jnp.where(p >= width - 2, late, jnp.where(at_edge, middle, inside))
+
+    def store(column, state):
         pairs = []
         for run, _, total, skew, green in state:
             pairs.append([encode(v, s) for v, s in zip((total + skew, green, total - skew, run), SCALES)])
         for channel in range(4):
             rows = jnp.concatenate([pairs[0][channel], pairs[1][channel]], axis=0)
-            coded[d, channel, x] = rows.astype(jnp.bfloat16)
-
-    def inner(d):
-        def column(x, _):
-            slab = 2 * d + x + 1
+            coded[column, channel] = rows.astype(jnp.bfloat16)
+
+    def send(column):
+        return pltpu.make_async_remote_copy(
+            coded.at[column], recv.at[me, lax.rem(column, 2)], ps_sem.at[column], pr_sem.at[me, lax.rem(column, 2)],
+            device_id={"depth": lax.div(column, 2)}, device_id_type=MESH,
+        )
+
+    def early(p, _):
+        slab = target(p) + 1
+        state = []
+        for h in range(2):
+            squared = cell(slab, 0, h) ** 2
+            run = squared * pltpu.reciprocal(1.0 + squared, approx=True)
+            state.append((run, jnp.exp2(run * (-rate)), zeros, zeros, zeros))
+        state = inner_layers(slab, state)
+        for h in range(2):
+            run, _, total, skew, green = state[h]
+            for channel, value in enumerate((total, skew, green, run)):
+                part[p, channel, h] = value
+        return 0
+
+    def early_end(i, _):
+        columns = [target(2 * i), target(2 * i + 1)]
+        for u, column in enumerate(columns):
+            p = 2 * i + u
             state = []
             for h in range(2):
-                squared = cell(slab, 0, h) ** 2
-                run = squared * pltpu.reciprocal(1.0 + squared, approx=True)
-                state.append((run, jnp.exp2(run * (-rate)), zeros, zeros, zeros))
-            state = inner_layers(slab, state)
-            for h in range(2):
-                run, _, total, skew, green = state[h]
-                for channel, value in enumerate((total, skew, green, run)):
-                    part[d, channel, x, h] = value
-            return 0
-
-        lax.fori_loop(0, 2, column, 0)
-
-    def outer(d):
-        for x in range(2):
-            slab = 2 * d + x + 1
+                total, skew, green = (part[p, channel, h] for channel in range(3))
+                state.append((zeros, 1.0, total, skew, green))
+            done = front_layer(column + 1, state)
             state = []
             for h in range(2):
-                total, skew, green, run = (part[d, channel, x, h] for channel in range(4))
-                state.append((zeros, 1.0, total, skew, green))
-            done = front_layer(slab, state)
-            state = []
-            for h in range(2):
-                run = part[d, 3, x, h]
+                run = part[p, 3, h]
                 state.append((run, jnp.exp2(run * (-rate)), *done[h][2:]))
-            store(d, x, back_layer(slab, state))
-
-    def whole(d):
-        def column(x, _):
-            slab = 2 * d + x + 1
-            state = front_layer(slab, [(zeros, 1.0, zeros, zeros, zeros)] * 2)
-            store(d, x, back_layer(slab, inner_layers(slab, state)))
-            return 0
-
-        lax.fori_loop(0, 2, column, 0)
-
-    def send(d):
-        return pltpu.make_async_remote_copy(
-            coded.at[d], recv.at[me], ps_sem.at[d], pr_sem.at[me],
-            device_id={"depth": d}, device_id_type=MESH,
-        )
-
-    codes = []
-    orders = plan(depths)
-    for s in range(depths):
-        codes.append(sum(orders[k][s] * depths**k for k in range(depths)))
-    power = choose(me, [depths**k for k in range(depths)])
-
-    def target(s):
-        return lax.rem(choose(s, codes) // power, depths)
-
-    def early(s, _):
-        inner(target(s))
-        return 0
-
-    def early_end(s, _):
-        d = target(s)
-        outer(d)
-        send(d).start()
-        return 0
-
-    def late(s, _):
-        @pl.when(s == EARLY)
+            store(column, back_layer(column + 1, state))
+        for column in columns:
+            send(column).start()
+        return 0
+
+    def late(p, _):
+        @pl.when(p == EDGE)
         def _():
             @pl.when(has_down)
             def _():
@@ -310,29 +276,31 @@
                 x_down.wait_recv()
                 relayout(cx + 1)
 
-
-        d = target(s)
-        whole(d)
-
-        @pl.when(s < depths - 1)
-        def _():
-            send(d).start()
+        column = target(p)
+        state = front_layer(column + 1, [(zeros, 1.0, zeros, zeros, zeros)] * 2)
+        store(column, back_layer(column + 1, inner_layers(column + 1, state)))
+
+        @pl.when(p < width - 2)
+        def _():
+            send(column).start()
 
         return 0
 
     lax.fori_loop(0, FIRST, early, 0)
     z_down.wait_recv()
     z_up.wait_recv()
-    lax.fori_loop(0, FIRST, early_end, 0)
-    lax.fori_loop(FIRST, depths, late, 0)
-    recv[me] = coded[me]
+    lax.fori_loop(0, FIRST // 2, early_end, 0)
+    lax.fori_loop(FIRST, width, late, 0)
+    for x in range(2):
+        recv[me, x] = coded[2 * me + x]
 
     for s in range(1, depths):
         source = lax.rem(me + s, depths)
-        pltpu.make_async_remote_copy(
-            coded.at[source], recv.at[source], ps_sem.at[source], pr_sem.at[source],
-            device_id={"depth": source}, device_id_type=MESH,
-        ).wait_recv()
+        for x in range(2):
+            pltpu.make_async_remote_copy(
+                coded.at[x], recv.at[source, x], ps_sem.at[x], pr_sem.at[source, x],
+                device_id={"depth": source}, device_id_type=MESH,
+            ).wait_recv()
 
     for x in range(2):
         run = jnp.zeros((16, 128), jnp.float32)
@@ -340,8 +308,8 @@
         for k in range(depths):
             light = jnp.exp2(run * (-rate))
             for channel in range(3):
-                colours[channel] += light * decode(recv[k, channel, x], SCALES[channel])
-            run = run + decode(recv[k, 3, x], SCALES[3])
+                colours[channel] += light * decode(recv[k, x, channel], SCALES[channel])
+            run = run + decode(recv[k, x, 3], SCALES[3])
         image = [0.5 * SHADE * colour for colour in colours] + [1.0 - jnp.exp2(run * (-rate))]
         for channel in range(4):
             for h in range(2):
@@ -354,7 +322,8 @@
     z_down.wait_send()
     z_up.wait_send()
     for s in range(1, depths):
-        send(lax.rem(me + s, depths)).wait_send()
+        for x in range(2):
+            send(2 * lax.rem(me + s, depths) + x).wait_send()
 
 
 def shards(volume):
@@ -371,10 +340,10 @@
             pltpu.VMEM((cx + 2, 2, LEAD + PITCH * cz, 128), jnp.float32),
             pltpu.VMEM((2, cx, 16, 128), jnp.bfloat16),
             pltpu.VMEM((2, cx, 16, 128), jnp.bfloat16),
-            pltpu.VMEM((depths, 4, 2, 2, 8, 128), jnp.float32),
-            pltpu.VMEM((depths, 4, 2, 16, 128), jnp.bfloat16),
-            pltpu.VMEM((depths, 4, 2, 16, 128), jnp.bfloat16),
-            dma((4,)), dma((2,)), dma((2,)), dma((2,)), dma((2,)), dma((depths,)), dma((depths,)),
+            pltpu.VMEM((FIRST, 4, 2, 8, 128), jnp.float32),
+            pltpu.VMEM((cx, 4, 16, 128), jnp.bfloat16),
+            pltpu.VMEM((depths, 2, 4, 16, 128), jnp.bfloat16),
+            dma((4,)), dma((2,)), dma((2,)), dma((2,)), dma((2,)), dma((cx,)), dma((depths, 2)),
         ],
         compiler_params=pltpu.CompilerParams(
             collective_id=0, has_side_effects=True, vmem_limit_bytes=52 * 1024 * 1024

time: 31 us -> 30.5 us (0.984)
  the two profiles are of different devices: /device:TPU:56 before, /device:TPU:40 now
where the time goes in v5:
time: 30.5 us; the launch traced here: 30.3 us
  Pallas kernels  29.7 us (97%)
  local copies, waits for them, and re-layouts  0.63 us (2%)
    pallas_call x1, Pallas kernels, shards(): pl.pallas_call(functools.partial(render_kernel, tiles, depths), out_shape...  29.7 us
    unnamed x1, local copies, waits for them, and re-layouts  0.63 us

profile of v5, /device:TPU:40, one launch (start us, length us, event | category | flops | bytes accessed | tf_op | source)
XLA Modules:
  0.0 30.3 jit_solution(6978243267936298289)
XLA Ops:
  0.0 29.7 %shard_map.17 = f32[4,2,2048]{2,1,0:T(2,128)S(1)} custom-call(bf16[16,32,2048]{2,1,0:T(8,128)(2,1)} %v_ref.1), custom_call_target="tpu_custom_call" | custom-call | flops 50000000 | bytes 2300000 | tf_op jit(solution)/shard_map/pallas_call | solution.py:333
  29.7 0.6 %copy.3 = f32[4,2,2048]{2,1,0:T(2,128)} copy(f32[4,2,2048]{2,1,0:T(2,128)S(1)} %shard_map.17) | data formatting | bytes 131072
